TPU v7x, 512 devices: a whole 4x8x8 slice. The times are simulated.
512 devices in a mesh: ctx: 64 (over z, y_lo, core), fsdp: 8 (over y_hi, x).
Axes of the slice: x: 4, y: 8 (y_hi: 2, y_lo: 4; y = y_hi * 4 + y_lo), z: 8, core: 2. Of those that a mesh axis runs over, the one named last changes fastest.
Arguments:
- hidden: bfloat16 [8, 8192, 2560], P('fsdp', 'ctx'), may hold values from -20 to 20
- queries: bfloat16 [8, 8192, 6144], P('fsdp', 'ctx'), may hold values from -6 to 6
- keys: bfloat16 [8, 8192, 512], P('fsdp', 'ctx'), may hold values from -6 to 6
- values: bfloat16 [8, 8192, 512], P('fsdp', 'ctx'), may hold values from -6 to 6
- out_grad: bfloat16 [8, 8192, 6144], P('fsdp', 'ctx'), may hold values from -10 to 10
- doc_ids: int32 [8, 8192], P('fsdp'), may hold values from 0 to 63, never falling along the last dimension, each value on 1 to 129 neighbouring positions
Outputs:
- kv_grads: bfloat16 [8, 8192, 1024], P('fsdp', 'ctx')
- updates: float32 [8, 2560, 128], P('fsdp', 'ctx')
Inputs may be any that keep to these rules, and one draw needn't show every extreme that they name: `doc_ids`: in each sequence ids never fall; each run of one id is a document of 1 to 129 positions, and at least one document has 129.
All inputs are finite; a program needn't handle non-finite values.
Results may differ from a plain program's by a relative error of at most 0.0056.
Values may be sent and summed in bfloat16 or wider, within the bound.
A program may use at most 128 MiB of HBM per device.

v0:
```python
import math

import jax
import jax.numpy as jnp
from jax import lax
from jax.sharding import PartitionSpec as P

D = 2560
KV_HEADS = 4
GROUP = 12
HEAD_DIM = 128
STEPS = 2
NS_ITERS = 5


coeff_a = 3.4445
coeff_b = -4.775
coeff_c = 2.0315


def passed_along(value, axis, by):
    size = lax.axis_size(axis)
    pairs = [(i, i + by) for i in range(size) if 0 <= i + by < size]
    return lax.ppermute(value, axis, pairs)


def window_mask(query_doc, key_doc, pad_len):
    row_index = lax.broadcasted_iota(jnp.int32, (query_doc.shape[0], key_doc.shape[0]), 0)
    col_index = lax.broadcasted_iota(jnp.int32, (query_doc.shape[0], key_doc.shape[0]), 1)
    same_doc = query_doc[:, None] == key_doc[None, :]
    return jnp.logical_and(same_doc, col_index <= row_index + pad_len)


def group_grads(q_group, g_group, k_group, v_group, visible):
    score_scale = 1.0 / math.sqrt(HEAD_DIM)
    scores = score_scale * jnp.einsum(
        "ihd,jd->hij", q_group, k_group, preferred_element_type=jnp.float32
    )
    masked = jnp.where(visible[None], scores, -1e30)
    row_max = jnp.max(masked, axis=-1, keepdims=True)
    exp_vals = jnp.where(visible[None], jnp.exp(masked - row_max), 0.0)
    attn_probs = exp_vals / jnp.sum(exp_vals, axis=-1, keepdims=True)
    prob_grad = jnp.einsum("ihd,jd->hij", g_group, v_group, preferred_element_type=jnp.float32)
    row_delta = jnp.sum(attn_probs * prob_grad, axis=-1, keepdims=True)
    score_low = (attn_probs * (prob_grad - row_delta)).astype(jnp.bfloat16)
    probs_low = attn_probs.astype(jnp.bfloat16)
    key_grad = score_scale * jnp.einsum(
        "hij,ihd->jd", score_low, q_group, preferred_element_type=jnp.float32
    )
    value_grad = jnp.einsum("hij,ihd->jd", probs_low, g_group, preferred_element_type=jnp.float32)
    return (key_grad, value_grad)


def newton_steps(ns_state, total_gram):
    for iteration in range(NS_ITERS):
        ns_gram = total_gram(
            jnp.einsum("mrd,mre->mde", ns_state, ns_state, precision=lax.Precision.HIGHEST)
        )
        squared = jnp.einsum("mde,mef->mdf", ns_gram, ns_gram, precision=lax.Precision.HIGHEST)
        poly_term = coeff_b * ns_gram + coeff_c * squared
        ns_state = coeff_a * ns_state + jnp.einsum(
            "mre,mde->mrd", ns_state, poly_term, precision=lax.Precision.HIGHEST
        )
    return math.sqrt(D) * ns_state


def shards(hidden, queries, keys, values, out_grad, doc_ids):
    tok_len = queries.shape[1]
    my_block = lax.axis_index("ctx")
    pad_len = (STEPS - 1) * tok_len
    kv_pair = jnp.stack([keys[0], values[0]])
    kv_stash = [kv_pair]
    step_idx = 1
    kv_pair = passed_along(kv_pair, "ctx", 1)
    kv_stash.append(kv_pair)
    kv_window = jnp.concatenate(kv_stash[::-1], axis=1)
    doc_row = doc_ids[0]
    doc_pad = jnp.concatenate([jnp.full((pad_len,), -1, jnp.int32), doc_row], axis=0)
    key_doc = lax.dynamic_slice_in_dim(doc_pad, my_block * tok_len, STEPS * tok_len, 0)
    query_doc = lax.dynamic_slice_in_dim(doc_row, my_block * tok_len, tok_len, 0)
    visible = window_mask(query_doc, key_doc, pad_len)
    q_blocks = queries[0].reshape(tok_len, KV_HEADS, GROUP, HEAD_DIM)
    g_blocks = out_grad[0].reshape(tok_len, KV_HEADS, GROUP, HEAD_DIM)
    k_window = kv_window[0].reshape(STEPS * tok_len, KV_HEADS, HEAD_DIM)
    v_window = kv_window[1].reshape(STEPS * tok_len, KV_HEADS, HEAD_DIM)
    key_parts = []
    value_parts = []
    for head_group in range(KV_HEADS):
        key_grad, value_grad = group_grads(
            q_blocks[:, head_group],
            g_blocks[:, head_group],
            k_window[:, head_group],
            v_window[:, head_group],
            visible,
        )
        key_parts.append(key_grad)
        value_parts.append(value_grad)
    contribs = jnp.concatenate(key_parts + value_parts, axis=1)
    pieces = [
        contribs[(STEPS - 1 - step_idx) * tok_len : (STEPS - step_idx) * tok_len]
        for step_idx in range(STEPS)
    ]
    totals = pieces[STEPS - 1]
    step_idx = 0
    totals = passed_along(totals, "ctx", -1) + pieces[step_idx]
    kv_grads = totals.astype(jnp.bfloat16)
    grad_term = jnp.einsum(
        "tf,tmh->mfh",
        hidden[0],
        kv_grads.reshape(tok_len, 2 * KV_HEADS, HEAD_DIM),
        preferred_element_type=jnp.float32,
    )
    row_pieces = lax.all_to_all(grad_term[None], "ctx", split_axis=2, concat_axis=0, tiled=True)
    weight_grad = lax.psum_scatter(
        jnp.sum(row_pieces, axis=0), "fsdp", scatter_dimension=0, tiled=True
    )
    full_mat = lax.all_gather(weight_grad, "ctx", axis=1, tiled=True)
    frob_norm = jnp.sqrt(jnp.sum(full_mat * full_mat, axis=(1, 2), keepdims=True))
    ns_final = newton_steps(full_mat / (frob_norm + 1e-07), lambda partial_value: partial_value)
    row_count = weight_grad.shape[1]
    updates = lax.dynamic_slice_in_dim(ns_final, my_block * row_count, row_count, 1)
    return (kv_grads[None], updates)


def solution(mesh):
    placed = (
        P("fsdp", "ctx", None),
        P("fsdp", "ctx", None),
        P("fsdp", "ctx", None),
        P("fsdp", "ctx", None),
        P("fsdp", "ctx", None),
        P("fsdp", None),
    )
    return jax.shard_map(
        shards,
        mesh=mesh,
        in_specs=placed,
        out_specs=(P("fsdp", "ctx", None), P("fsdp", "ctx", None)),
        check_vma=False,
    )
```

profile of v0, /device:TPU:7, one launch (start us, length us, event | category | flops | bytes accessed | tf_op | source)
XLA Modules:
  0.0 568.4 jit_solution(11944197709671205479)
XLA Ops:
  7.2 1.1 copy.63
  8.3 1.0 copy.64
  9.4 3.8 collective-permute-start
  14.6 2.7 copy.66
  17.3 1.6 copy.69
  19.2 1.2 copy-done.3
  20.4 1.8 fusion.92
  22.2 1.8 fusion.91
  24.0 1.8 fusion.90
  25.9 3.0 fusion.93
  28.9 1.9 fusion.15
  32.7 1.0 copy-done.9
  34.1 1.0 copy-done.4
  39.4 1.9 collective-permute-start.1
  41.4 8.6 %collective-permute-done.1 = f32[128,1024]{0,1:T(8,128)S(1)} collective-permute-done((f32[128,1024]{0,1:T(8,128)S(1)}, f32[128,1024]{0,1:T(8,128)S(1)}, u32[]{:S(2)}, u32[]{:S(2)}) %collective-permute-start.1) | collective-permute-done | bytes 524320 | tf_op jit(solution)/shard_map/ppermute | solution.py:24
  50.0 5.4 convolution_bitcast_fusion
  55.4 11.4 %copy.99 = f32[1,8,2560,128]{3,1,0,2:T(8,128)} copy(f32[1,8,2560,128]{2,3,1,0:T(8,128)} %convolution_bitcast_fusion) | data formatting | bytes 20971520 | tf_op jit(solution)/shard_map/broadcast_in_dim | solution.py:113
  66.8 251.1 %all_to_all.12 = f32[1,8,2560,128]{3,1,0,2:T(8,128)} all-to-all(f32[1,8,2560,128]{3,1,0,2:T(8,128)} %copy.99), channel_id=1, replica_groups=mesh['ctx'=64,'fsdp'=8] {'ctx'}, dimensions={2} | all-to-all | bytes 20971520 | tf_op jit(solution)/shard_map/all_to_all | solution.py:113
  317.9 4.5 reduce.4
  323.4 95.7 %reduce-scatter.4.cloned.1.call-done = f32[1,40,128]{2,1,0:T(8,128)} async-done(((f32[8,40,128]{2,1,0:T(8,128)}), f32[1,40,128]{2,1,0:T(8,128)}) %reduce-scatter.4.cloned.1.call-update) | async-done | bytes 20496
  420.0 117.7 %all-gather.2.cloned.1.call-done = f32[1,2560,128]{2,1,0:T(8,128)} async-done(((f32[1,40,128]{2,1,0:T(8,128)}), f32[1,2560,128]{2,1,0:T(8,128)}) %all-gather.2.cloned.1.call-update) | async-done | bytes 1310736 | tf_op jit(solution)/shard_map/all_gather | solution.py:117
  537.7 2.3 multiply_reduce_fusion
  540.6 4.1 fusion.37
  544.9 1.2 fusion.4
  546.1 2.2 fusion.34
  548.6 1.2 fusion.5
  549.8 2.2 fusion.31
  552.2 1.2 fusion.6
  553.4 2.4 fusion.28
  556.1 1.2 fusion.7
  557.3 2.2 fusion.25
  559.7 1.2 convolution_bitcast_fusion.1
  (50 shorter events, 11.7 us)
Async XLA Ops:
  7.2 42.9 %copy-start = (bf16[1,128,2560]{2,1,0:T(8,128)(2,1)S(1)}, bf16[1,128,2560]{2,1,0:T(8,128)(2,1)}, u32[]{:S(2)}) copy-start(bf16[1,128,2560]{2,1,0:T(8,128)(2,1)} %param.6) | copy-start | bytes 1966084
  7.2 411.9 %reduce-scatter.4.cloned.1.call-start = ((), (), s32[]{:S(2)}) async-start(), calls=%async_computation.3 | async-start | bytes 184320
  9.4 9.7 %collective-permute-start = (bf16[2,128,512]{1,2,0:T(8,128)(2,1)S(1)}, bf16[2,128,512]{1,2,0:T(8,128)(2,1)S(1)}, u32[]{:S(2)}, u32[]{:S(2)}) collective-permute-start(bf16[2,128,512]{1,2,0:T(8,128)(2,1)S(1)} %pad_maximum_fusion), channel_id=1, source_target_pairs={{0,8},{8,16},{16,24},{24,32},{32,40},{40,48},{48,56},{56,64},{64,7... | collective-permute-start | bytes 786440 | tf_op jit(solution)/shard_map/ppermute | solution.py:24
  14.6 2.7 copy-start.1
  19.0 1.4 copy-start.3
  25.9 3.1 copy-start.2
  28.9 1.9 copy-start.8
  30.9 1.4 copy-start.7
  32.3 1.4 copy-start.9
  33.7 1.4 copy-start.4
  35.5 1.4 copy-start.6
  39.4 10.5 %collective-permute-start.1 = (f32[128,1024]{0,1:T(8,128)S(1)}, f32[128,1024]{0,1:T(8,128)S(1)}, u32[]{:S(2)}, u32[]{:S(2)}) collective-permute-start(f32[128,1024]{0,1:T(8,128)S(1)} %slice.98), channel_id=1, source_target_pairs={{8,0},{16,8},{24,16},{32,24},{40,32},{48,40},{56,48},{64,56},{72,6... | collective-permute-start | bytes 1572872 | tf_op jit(solution)/shard_map/ppermute | solution.py:24
  323.1 214.5 %all-gather.2.cloned.1.call-start = ((), (), s32[]{:S(2)}) async-start(), calls=%async_computation.2 | async-start | bytes 1331200 | tf_op jit(solution)/shard_map/all_gather | solution.py:117
  540.6 4.3 copy-start.5
Sparse Core Ops, SparseCore 0:
  323.3 95.7 reduce-scatter.3
  421.5 116.1 all-gather.1
where the time goes:
time: 570 us; the launch traced here: 568 us
  blocking collectives  251 us (44%)
  waiting for transfers between devices  222 us (39%)
  matrix products  40.5 us (7%)
  local copies, waits for them, and re-layouts  26.1 us (5%)
  between operations  15.1 us (3%)
  other arithmetic  7.61 us (1%)
  starting transfers between devices  5.95 us (1%)
    all_to_all x1, blocking collectives, shards(): lax.all_to_all(grad_term[None], 'ctx', split_axis=2, concat_axis=0, tiled...  251 us
    all_gather x1, waiting for transfers between devices, shards(): full_mat = lax.all_gather(weight_grad, 'ctx', axis=1, tiled=True)  118 us
    unnamed x3, waiting for transfers between devices  95.8 us
    dot_general x5, matrix products, newton_steps(): jnp.einsum('mrd,mre->mde', ns_state, ns_state, precision=lax.Precision.HI...  13.2 us
    unnamed x26, local copies, waits for them, and re-layouts  13.2 us
    broadcast_in_dim x1, local copies, waits for them, and re-layouts, shards(): grad_term[None]  11.4 us
  transfers between devices with their start and end apart: 4, of which 3 were waited for; matrix products, arithmetic and copies ran while one was open for 1% of the time, Pallas kernels for 0%

commit v1 on v0

v1 whole, which is shorter than its diff:
```python
import math

import jax
import jax.numpy as jnp
from jax import lax
from jax.experimental import pallas as pl
from jax.experimental.pallas import tpu as pltpu
from jax.sharding import PartitionSpec as P

D = 2560
KV_HEADS = 4
GROUP = 12
HEAD_DIM = 128
NS_ITERS = 5
TOK = 128
X, Y, Z, YL = 4, 8, 8, 4
QUARTER = D // X
CHUNK = QUARTER // Y
ROWS = CHUNK // 2
HEADS_W = GROUP * HEAD_DIM
KV_W = KV_HEADS * HEAD_DIM

coeff_a = 3.4445
coeff_b = -4.775
coeff_c = 2.0315

F32 = jnp.float32
BF16 = jnp.bfloat16
MESH = pl.DeviceIdType.MESH
HIGHEST = lax.Precision.HIGHEST


def device(x, yh, yl, z, core):
    return {"ctx": z * 8 + yl * 2 + core, "fsdp": yh * 4 + x}


def remote(src, dst, send, recv, to):
    return pltpu.make_async_remote_copy(
        src_ref=src, dst_ref=dst, send_sem=send, recv_sem=recv, device_id=to, device_id_type=MESH
    )


def mm(a, b, dims, **kw):
    return lax.dot_general(a, b, ((dims[0], dims[1]), ((), ())), preferred_element_type=F32, **kw)


def kernel(
    hid, qs, ks, vs, og, docs, kv_out, up_out,
    q_v, g_v, kwin, bias, acck, accv, csend, cown, crecv, kvb, hall, ht, kall, w32, wlo,
    yrecv, zsend, zrecv, gpart, g1buf, s1, g2buf, gfull,
    loc, kvs, kvr, hs, hr, cs, cr, xs, xr, ys, yr, zs, zr, g1s, g1r, g2s, g2r, g3s, g3r, outs,
):
    ctx, fsdp = lax.axis_index("ctx"), lax.axis_index("fsdp")
    z, yl, core = ctx // 8, lax.rem(ctx // 2, YL), lax.rem(ctx, 2)
    yh, x = fsdp // X, lax.rem(fsdp, X)
    y = yh * YL + yl
    other = 1 - core
    nxt, prv = lax.rem(ctx + 1, 64), lax.rem(ctx + 63, 64)

    def load_q(g):
        cols = slice(g * HEADS_W, (g + 1) * HEADS_W)
        return (
            pltpu.make_async_copy(qs.at[0, :, cols], q_v.at[:, cols], loc.at[g]),
            pltpu.make_async_copy(og.at[0, :, cols], g_v.at[:, cols], loc.at[4 + g]),
        )

    own_k = pltpu.make_async_copy(ks.at[0], kwin.at[0, 1], loc.at[8])
    own_v = pltpu.make_async_copy(vs.at[0], kwin.at[1, 1], loc.at[9])
    own_h = pltpu.make_async_copy(hid.at[0, :, pl.ds(pl.multiple_of(x * QUARTER, 128), QUARTER)], hall.at[0], loc.at[10])
    own_k.start()
    own_v.start()
    for g in range(KV_HEADS):
        for c in load_q(g):
            c.start()
    own_h.start()

    cell = yl * 2 + core

    def x_dev(dx, dc):
        return device(lax.rem(x + dx, X), yh, yl, z, lax.rem(core + dc, 2))

    def y_dev(k):
        to = lax.rem(y + k, Y)
        return device(x, to // YL, lax.rem(to, YL), z, core)

    def cell_dev(k):
        to = lax.rem(cell + k, 8)
        return {"ctx": z * 8 + to, "fsdp": fsdp}

    def z_dev(k):
        return {"ctx": lax.rem(z + k, Z) * 8 + cell, "fsdp": fsdp}

    def owner(g, half):
        return device(g, core, yl, 2 * x + yh, half)

    selfish = jnp.logical_and(core == yh, z == 2 * x + yh)
    barrier = pltpu.get_barrier_semaphore()

    def greet(to):
        pl.semaphore_signal(barrier, inc=1, device_id=to, device_id_type=MESH)

    count = 0
    for to in ({"ctx": nxt, "fsdp": fsdp}, {"ctx": prv, "fsdp": fsdp}):
        greet(to)
        count += 1
    for k in range(1, 8):
        greet(x_dev(k // 2, k % 2))
        greet(y_dev(k))
        greet(cell_dev(k))
        greet(z_dev(k))
        count += 4
    for k in range(Z):
        src = device(z // 2, lax.rem(z, 2), yl, lax.rem(z + k, Z), yh)
        if k == 0:
            @pl.when(jnp.logical_not(selfish))
            def _():
                greet(src)
        else:
            greet(src)
        count += 1

    eye = lax.broadcasted_iota(jnp.int32, (TOK, TOK), 0) == lax.broadcasted_iota(jnp.int32, (TOK, TOK), 1)
    own_row = docs[:, pl.ds(pl.multiple_of(ctx * TOK, TOK), TOK)].astype(F32)
    prv_row = docs[:, pl.ds(pl.multiple_of(prv * TOK, TOK), TOK)].astype(F32)
    prv_row = jnp.where(ctx == 0, -1.0, prv_row)

    def as_column(row):
        return jnp.sum(jnp.where(eye, jnp.broadcast_to(row, (TOK, TOK)), 0.0), axis=1, keepdims=True)

    earlier = lax.broadcasted_iota(jnp.int32, (TOK, TOK), 0) <= lax.broadcasted_iota(jnp.int32, (TOK, TOK), 1)
    bias[0:TOK, :] = jnp.where(as_column(prv_row) == own_row, 0.0, -1e30)
    bias[TOK:, :] = jnp.where(jnp.logical_and(as_column(own_row) == own_row, earlier), 0.0, -1e30)

    pl.semaphore_wait(barrier, count - selfish.astype(jnp.int32))

    send_k = remote(ks.at[0], kwin.at[0, 0], kvs.at[0], kvr.at[0], {"ctx": nxt, "fsdp": fsdp})
    send_v = remote(vs.at[0], kwin.at[1, 0], kvs.at[1], kvr.at[1], {"ctx": nxt, "fsdp": fsdp})
    send_k.start()
    send_v.start()

    def hidden_cols(which):
        return hid.at[0, :, pl.ds(pl.multiple_of(which * QUARTER, 128), QUARTER)]

    send_h = [
        remote(hidden_cols(lax.rem(x + dx, X)), hall.at[2 * dx], hs.at[2 * dx], hr.at[2 * dx], x_dev(dx, 0))
        for dx in range(1, X)
    ]
    send_h.append(remote(hidden_cols(x), hall.at[1], hs.at[1], hr.at[1], x_dev(0, 1)))
    for c in send_h:
        c.start()
    forward_h = [
        remote(hall.at[2 * dx], hall.at[2 * dx + 1], hs.at[2 * dx + 1], hr.at[2 * dx + 1], x_dev(0, 1))
        for dx in range(1, X)
    ]

    scale = 1.0 / math.sqrt(HEAD_DIM)
    scale2 = scale * math.log2(math.e)

    def attention(g):
        for c in load_q(g):
            c.wait()
        lanes = slice(g * HEAD_DIM, (g + 1) * HEAD_DIM)
        kw = kwin[0, :, :, lanes].reshape(2 * TOK, HEAD_DIM)
        vw = kwin[1, :, :, lanes].reshape(2 * TOK, HEAD_DIM)
        acck[...] = jnp.zeros_like(acck)
        accv[...] = jnp.zeros_like(accv)

        def pair(i, _):
            at = [pl.ds(pl.multiple_of((g * GROUP + 2 * i + j) * HEAD_DIM, HEAD_DIM), HEAD_DIM) for j in range(2)]
            q2 = jnp.concatenate([q_v[:, at[0]], q_v[:, at[1]]], axis=0)
            g2 = jnp.concatenate([g_v[:, at[0]], g_v[:, at[1]]], axis=0)
            both = jnp.concatenate([bias[...], bias[...]], axis=1)
            s = mm(kw, q2, ((1,), (1,))) * scale2 + both
            dp = mm(vw, g2, ((1,), (1,)))
            e = jnp.exp2(s - jnp.max(s, axis=0, keepdims=True))
            inv = 1.0 / jnp.sum(e, axis=0, keepdims=True)
            p = e * inv
            delta = jnp.sum(p * dp, axis=0, keepdims=True)
            ds = (p * (dp - delta)).astype(BF16)
            acck[...] += mm(ds, q2, ((1,), (0,)))
            accv[...] += mm(p.astype(BF16), g2, ((1,), (0,)))
            return 0

        lax.fori_loop(0, GROUP // 2, pair, 0)
        csend[g, 0] = acck[0:TOK, :] * scale
        csend[g, 1] = accv[0:TOK, :]
        cown[g, 0] = acck[TOK:, :] * scale
        cown[g, 1] = accv[TOK:, :]

    def contribs(g):
        return remote(csend.at[g], crecv.at[g], cs.at[g], cr.at[g], {"ctx": prv, "fsdp": fsdp})

    def x_copies(g):
        return [
            remote(
                kvb.at[g, lax.rem(core + k % 2, 2)], kall.at[g, k], xs.at[g, k], xr.at[g, k], x_dev(k // 2, k % 2)
            )
            for k in (1, 2, 4, 6, 3, 5, 7)
        ]

    def out_copies(g):
        return [
            pltpu.make_async_copy(
                kvb.at[g, j], kv_out.at[0, :, pl.ds(j * KV_W + g * HEAD_DIM, HEAD_DIM)], outs.at[2 * g + j]
            )
            for j in range(2)
        ]

    def finish(g):
        contribs(g).wait_recv()
        kvb[g] = (crecv[g] + cown[g]).astype(BF16)
        for c in x_copies(g):
            c.start()
        kall[g, 0] = kvb[g, core]
        for c in out_copies(g):
            c.start()

    def y_copies(g):
        return [
            remote(wlo.at[g, lax.rem(y + k, Y)], yrecv.at[g, k], ys.at[g, k], yr.at[g, k], y_dev(k))
            for k in (4, 3, 5, 2, 6, 1, 7)
        ]

    def product(g):
        for c in x_copies(g):
            c.wait_recv()
        w = mm(ht[...], kall[g].reshape(8 * TOK, HEAD_DIM), ((1,), (0,))).reshape(Y, CHUNK, HEAD_DIM)
        wlo[g] = w.astype(BF16)
        for c in y_copies(g):
            c.start()
        w32[g] = w

    def z_copy(g, half):
        return remote(zsend.at[g, half], zrecv.at[z], zs.at[g, half], zr.at[z], owner(g, half))

    def z_local(g, half):
        return pltpu.make_async_copy(zsend.at[g, half], zrecv.at[z], zr.at[z])

    def is_mine(g, half):
        return jnp.logical_and(selfish, jnp.logical_and(x == g, core == half))

    def y_sum(g):
        for c in y_copies(g):
            c.wait_recv()
        total = w32[g, y]
        for k in range(1, Y):
            total = total + yrecv[g, k].astype(F32)
        zsend[g] = total.reshape(2, ROWS, HEAD_DIM)
        for half in range(2):
            mine = is_mine(g, half)

            @pl.when(mine)
            def _(half=half):
                z_local(g, half).start()

            @pl.when(jnp.logical_not(mine))
            def _(half=half):
                z_copy(g, half).start()

    own_k.wait()
    own_v.wait()
    send_k.wait_recv()
    send_v.wait_recv()
    attention(0)
    contribs(0).start()
    for c in send_h[:3]:
        c.wait_recv()
    for c in forward_h:
        c.start()
    attention(1)
    contribs(1).start()
    finish(0)
    own_h.wait()
    send_h[3].wait_recv()
    for c in forward_h:
        c.wait_recv()
    for k in range(8):
        ht[:, k * TOK:(k + 1) * TOK] = hall[k].T
    attention(2)
    contribs(2).start()
    finish(1)
    product(0)
    attention(3)
    contribs(3).start()
    finish(2)
    product(1)
    y_sum(0)
    finish(3)
    product(2)
    y_sum(1)
    product(3)
    y_sum(2)
    y_sum(3)

    send_k.wait_send()
    send_v.wait_send()
    for c in send_h + forward_h:
        c.wait_send()
    for g in range(KV_HEADS):
        contribs(g).wait_send()
        for c in x_copies(g) + y_copies(g):
            c.wait_send()
        for c in out_copies(g):
            c.wait()
        for half in range(2):
            @pl.when(jnp.logical_not(is_mine(g, half)))
            def _(half=half):
                z_copy(g, half).wait_send()

    for k in range(Z):
        pltpu.make_async_copy(zrecv.at[k], zrecv.at[k], zr.at[k]).wait()
    w = zrecv[0]
    for k in range(1, Z):
        w = w + zrecv[k]

    gpart[...] = mm(w, w, ((0,), (0,)), precision=HIGHEST).reshape(8, 16, HEAD_DIM)
    step1 = [
        remote(gpart.at[lax.rem(cell + k, 8)], g1buf.at[k], g1s.at[k], g1r.at[k], cell_dev(k)) for k in range(1, 8)
    ]
    for c in step1:
        c.start()
    total = gpart[cell]
    for c in step1:
        c.wait_recv()
    for k in range(1, 8):
        total = total + g1buf[k]
    s1[...] = total
    step2 = [remote(s1, g2buf.at[k], g2s.at[k], g2r.at[k], z_dev(k)) for k in range(1, 8)]
    for c in step2:
        c.start()
    for c in step1:
        c.wait_send()
    for c in step2:
        c.wait_recv()
    for k in range(1, 8):
        total = total + g2buf[k]
    gfull[cell] = total
    step3 = [remote(gfull.at[cell], gfull.at[cell], g3s.at[k], g3r.at[k], cell_dev(k)) for k in range(1, 8)]
    for c in step3:
        c.start()
    for c in step2:
        c.wait_send()
    for c in step3:
        c.wait_recv()
    gram = gfull[...].reshape(HEAD_DIM, HEAD_DIM)

    ident = jnp.where(eye, 1.0, 0.0)
    norm = jnp.sqrt(jnp.sum(jnp.sum(gram * ident, axis=1, keepdims=True), axis=0, keepdims=True))
    inv = 1.0 / (norm + 1e-07)
    gram = gram * inv * inv

    def dot(a, b):
        return mm(a, b, ((1,), (0,)), precision=HIGHEST)

    run = None
    for it in range(NS_ITERS):
        poly = coeff_a * ident + coeff_b * gram + coeff_c * dot(gram, gram)
        run = poly if run is None else dot(run, poly)
        if it < NS_ITERS - 1:
            gram = dot(dot(poly, gram), poly)
    up_out[0] = dot(w * (inv * math.sqrt(D)), run)
    for c in step3:
        c.wait_send()


def shards(hidden, queries, keys, values, out_grad, doc_ids):
    any_spec = pl.BlockSpec(memory_space=pl.ANY)
    vmem = pl.BlockSpec(memory_space=pltpu.VMEM)
    dma = pltpu.SemaphoreType.DMA
    heads = KV_HEADS
    return pl.pallas_call(
        kernel,
        out_shape=(
            jax.ShapeDtypeStruct((1, TOK, 2 * KV_W), BF16),
            jax.ShapeDtypeStruct((1, ROWS, HEAD_DIM), F32),
        ),
        in_specs=[any_spec] * 5 + [vmem],
        out_specs=(any_spec, vmem),
        scratch_shapes=[
            pltpu.VMEM((TOK, heads * HEADS_W), BF16),
            pltpu.VMEM((TOK, heads * HEADS_W), BF16),
            pltpu.VMEM((2, 2, TOK, KV_W), BF16),
            pltpu.VMEM((2 * TOK, TOK), F32),
            pltpu.VMEM((2 * TOK, HEAD_DIM), F32),
            pltpu.VMEM((2 * TOK, HEAD_DIM), F32),
            pltpu.VMEM((heads, 2, TOK, HEAD_DIM), F32),
            pltpu.VMEM((heads, 2, TOK, HEAD_DIM), F32),
            pltpu.VMEM((heads, 2, TOK, HEAD_DIM), F32),
            pltpu.VMEM((heads, 2, TOK, HEAD_DIM), BF16),
            pltpu.VMEM((8, TOK, QUARTER), BF16),
            pltpu.VMEM((QUARTER, 8 * TOK), BF16),
            pltpu.VMEM((heads, 8, TOK, HEAD_DIM), BF16),
            pltpu.VMEM((heads, Y, CHUNK, HEAD_DIM), F32),
            pltpu.VMEM((heads, Y, CHUNK, HEAD_DIM), BF16),
            pltpu.VMEM((heads, Y, CHUNK, HEAD_DIM), BF16),
            pltpu.VMEM((heads, 2, ROWS, HEAD_DIM), F32),
            pltpu.VMEM((Z, ROWS, HEAD_DIM), F32),
            pltpu.VMEM((8, 16, HEAD_DIM), F32),
            pltpu.VMEM((8, 16, HEAD_DIM), F32),
            pltpu.VMEM((16, HEAD_DIM), F32),
            pltpu.VMEM((8, 16, HEAD_DIM), F32),
            pltpu.VMEM((8, 16, HEAD_DIM), F32),
            dma((11,)),
            dma((2,)), dma((2,)),
            dma((8,)), dma((8,)),
            dma((heads,)), dma((heads,)),
            dma((heads, 8)), dma((heads, 8)),
            dma((heads, 8)), dma((heads, 8)),
            dma((heads, 2)), dma((Z,)),
            dma((8,)), dma((8,)),
            dma((8,)), dma((8,)),
            dma((8,)), dma((8,)),
            dma((8,)),
        ],
        compiler_params=pltpu.CompilerParams(
            collective_id=0, has_side_effects=True, vmem_limit_bytes=40 * 1024 * 1024
        ),
        name="muon_kv_grads",
    )(hidden, queries, keys, values, out_grad, doc_ids)


def solution(mesh):
    placed = (P("fsdp", "ctx", None),) * 5 + (P("fsdp", None),)
    return jax.shard_map(
        shards,
        mesh=mesh,
        in_specs=placed,
        out_specs=(P("fsdp", "ctx", None), P("fsdp", "ctx", None)),
        check_vma=False,
    )
```

time: 570 us -> 92.6 us (0.16)
  blocking collectives: 251 us -> 0 us
  waiting for transfers between devices: 222 us -> 0 us
  Pallas kernels: 0 us -> 83.9 us
  matrix products: 40.5 us -> 0 us
  local copies, waits for them, and re-layouts: 26.1 us -> 7.77 us
  between operations: 15.1 us -> 0.65 us
  other arithmetic: 7.61 us -> 0 us
  starting transfers between devices: 5.95 us -> 0 us
    all_to_all x1 -> x0, blocking collectives: 251 us -> none  [shards(): lax.all_to_all(grad_term[None], 'ctx', split_axis=2, concat_axis=0, tiled...]
    all_gather x1 -> x0, waiting for transfers between devices: 118 us -> none  [shards(): full_mat = lax.all_gather(weight_grad, 'ctx', axis=1, tiled=True)]
    unnamed x3 -> x0, waiting for transfers between devices: 95.8 us -> none
    pallas_call x0 -> x1, Pallas kernels: none -> 83.9 us  [shards(): pl.pallas_call(kernel, out_shape=(jax.ShapeDtypeStruct((1, TOK, 2 * KV_W)...]
    dot_general x28 -> x0, matrix products: 31.9 us -> none  [the longest x5 13.2 us: newton_steps(): jnp.einsum('mrd,mre->mde', ns_state, ns_state, precision=lax.Precision.HI...]
    broadcast_in_dim x1 -> x0, local copies, waits for them, and re-layouts: 11.4 us -> none  [shards(): grad_term[None]]
    ppermute x2 -> x0, waiting for transfers between devices: 8.57 us -> none  [passed_along(): return lax.ppermute(value, axis, pairs)]
    sub x4 -> x0, matrix products: 8.57 us -> none  [group_grads(): exp_vals = jnp.where(visible[None], jnp.exp(masked - row_max), 0.0)]
  transfers between devices with their start and end apart: 4 -> 0, of which waited for: 3 -> 0; matrix products, arithmetic and copies ran while one was open for 1% -> 0% of each run, Pallas kernels for 0% -> 0%
where the time goes in v1:
time: 92.6 us; the launch traced here: 92.3 us
  Pallas kernels  83.9 us (91%)
  local copies, waits for them, and re-layouts  7.77 us (8%)
    pallas_call x1, Pallas kernels, shards(): pl.pallas_call(kernel, out_shape=(jax.ShapeDtypeStruct((1, TOK, 2 * KV_W)...  83.9 us
    unnamed x14, local copies, waits for them, and re-layouts  7.77 us

profile of v1, /device:TPU:7, one launch (start us, length us, event | category | flops | bytes accessed | tf_op | source)
XLA Modules:
  0.0 92.3 jit_solution(15952266165494099043)
XLA Ops:
  0.6 0.0 copy-start
  0.6 1.4 %copy-done = bf16[1,128,6144]{2,1,0:T(8,128)(2,1)S(1)} copy-done((bf16[1,128,6144]{2,1,0:T(8,128)(2,1)S(1)}, bf16[1,128,6144]{2,1,0:T(8,128)(2,1)}, u32[]{:S(2)}) %copy-start) | copy-done | bytes 1572888
  2.0 0.0 copy-start.1
  2.0 1.4 %copy-done.1 = bf16[1,128,6144]{2,1,0:T(8,128)(2,1)S(1)} copy-done((bf16[1,128,6144]{2,1,0:T(8,128)(2,1)S(1)}, bf16[1,128,6144]{2,1,0:T(8,128)(2,1)}, u32[]{:S(2)}) %copy-start.1) | copy-done | bytes 1572888
  3.4 0.0 copy-start.2
  3.5 1.1 %copy-done.2 = bf16[1,128,2560]{2,1,0:T(8,128)(2,1)S(1)} copy-done((bf16[1,128,2560]{2,1,0:T(8,128)(2,1)S(1)}, bf16[1,128,2560]{2,1,0:T(8,128)(2,1)}, u32[]{:S(2)}) %copy-start.2) | copy-done | bytes 655384
  4.5 0.0 copy-start.3
  4.5 0.9 copy-done.3
  5.4 0.0 copy-start.4
  5.4 0.9 copy-done.4
  6.3 0.0 copy-start.5
  6.3 0.8 copy-done.5
  7.1 83.9 %muon_kv_grads.1 = (bf16[1,128,1024]{2,1,0:T(8,128)(2,1)S(1)}, f32[1,40,128]{2,1,0:T(8,128)S(1)}) custom-call(bf16[1,128,2560]{2,1,0:T(8,128)(2,1)S(1)} %copy-done.2, bf16[1,128,6144]{2,1,0:T(8,128)(2,1)S(1)} %copy-done, bf16[1,128,512]{2,1,0:T(8,128)(2,1)S(1)} %copy-done.3, bf16[1,128,512]{2,1,0:T(8,128)(2,1)S(1)} %copy-done.4, ...), custom_call_target="tpu_custom_call" | custom-call | tf_op jit(solution)/shard_map/muon_kv_grads/pallas_call | solution.py:371
  91.0 0.7 copy.10
  91.7 0.6 copy.11
Async XLA Ops:
  0.6 1.4 %copy-start = (bf16[1,128,6144]{2,1,0:T(8,128)(2,1)S(1)}, bf16[1,128,6144]{2,1,0:T(8,128)(2,1)}, u32[]{:S(2)}) copy-start(bf16[1,128,6144]{2,1,0:T(8,128)(2,1)} %qs.1) | copy-start | bytes 4718596
  2.0 1.4 %copy-start.1 = (bf16[1,128,6144]{2,1,0:T(8,128)(2,1)S(1)}, bf16[1,128,6144]{2,1,0:T(8,128)(2,1)}, u32[]{:S(2)}) copy-start(bf16[1,128,6144]{2,1,0:T(8,128)(2,1)} %og.1) | copy-start | bytes 4718596
  3.4 1.1 %copy-start.2 = (bf16[1,128,2560]{2,1,0:T(8,128)(2,1)S(1)}, bf16[1,128,2560]{2,1,0:T(8,128)(2,1)}, u32[]{:S(2)}) copy-start(bf16[1,128,2560]{2,1,0:T(8,128)(2,1)} %hid.1) | copy-start | bytes 1966084
  4.5 0.9 copy-start.3
  5.4 0.9 copy-start.4
  6.3 0.8 copy-start.5

commit v2 on v1

v2 whole, which is shorter than its diff:
```python
import math

import jax
import jax.numpy as jnp
from jax import lax
from jax.experimental import pallas as pl
from jax.experimental.pallas import tpu as pltpu
from jax.sharding import PartitionSpec as P

D = 2560
KV_HEADS = 4
GROUP = 12
HEAD_DIM = 128
NS_ITERS = 5
TOK = 128
X, Y, Z, YL = 4, 8, 8, 4
QUARTER = D // X
CHUNK = QUARTER // Y
ROWS = CHUNK // 2
HEADS_W = GROUP * HEAD_DIM
KV_W = KV_HEADS * HEAD_DIM

coeff_a = 3.4445
coeff_b = -4.775
coeff_c = 2.0315

F32 = jnp.float32
BF16 = jnp.bfloat16
MESH = pl.DeviceIdType.MESH
HIGHEST = lax.Precision.HIGHEST


def device(x, yh, yl, z, core):
    return {"ctx": z * 8 + yl * 2 + core, "fsdp": yh * 4 + x}


def remote(src, dst, send, recv, to):
    return pltpu.make_async_remote_copy(
        src_ref=src, dst_ref=dst, send_sem=send, recv_sem=recv, device_id=to, device_id_type=MESH
    )


def mm(a, b, dims, **kw):
    return lax.dot_general(a, b, ((dims[0], dims[1]), ((), ())), preferred_element_type=F32, **kw)


def wait_bytes(ref, sem):
    pltpu.make_async_copy(ref, ref, sem).wait()


def kernel(
    hid, qs, ks, vs, og, docs, kv_out, up_out,
    q_v, g_v, kwin, bias, qst, gst, dsb, pbb, csend, cown, crecv, kvb, hall, ht, kall, w32, wlo,
    yrecv, zsend, zrecv, gpart, g1buf, s1, g2buf, gfull,
    loc, loh, kvs, kvr, hs, hr, cs, cr, xs, xr, ys, yr, zs, zr, g1s, g1r, g2s, g2r, g3s, g3r, outs,
):
    ctx, fsdp = lax.axis_index("ctx"), lax.axis_index("fsdp")
    z, yl, core = ctx // 8, lax.rem(ctx // 2, YL), lax.rem(ctx, 2)
    yh, x = fsdp // X, lax.rem(fsdp, X)
    y = yh * YL + yl
    cell = yl * 2 + core
    nxt, prv = lax.rem(ctx + 1, 64), lax.rem(ctx + 63, 64)

    def x_dev(dx, dc):
        return device(lax.rem(x + dx, X), yh, yl, z, lax.rem(core + dc, 2))

    def y_dev(k):
        to = lax.rem(y + k, Y)
        return device(x, to // YL, lax.rem(to, YL), z, core)

    def cell_dev(k):
        return {"ctx": z * 8 + lax.rem(cell + k, 8), "fsdp": fsdp}

    def z_dev(k):
        return {"ctx": lax.rem(z + k, Z) * 8 + cell, "fsdp": fsdp}

    def owner(g, half):
        return device(g, core, yl, 2 * x + yh, half)

    selfish = jnp.logical_and(core == yh, z == 2 * x + yh)
    barrier = pltpu.get_barrier_semaphore()

    def greet(to):
        pl.semaphore_signal(barrier, inc=1, device_id=to, device_id_type=MESH)

    greet({"ctx": nxt, "fsdp": fsdp})
    greet({"ctx": prv, "fsdp": fsdp})
    for k in range(1, 8):
        greet(x_dev(k % 4, k // 4))
        greet(y_dev(k))
        greet(cell_dev(k))
        greet(z_dev(k))
    sources = [device(z // 2, lax.rem(z, 2), yl, lax.rem(z + k, Z), yh) for k in range(Z)]

    @pl.when(jnp.logical_not(selfish))
    def _():
        greet(sources[0])

    for src in sources[1:]:
        greet(src)
    greeted = 2 + 4 * 7 + Z - selfish.astype(jnp.int32)

    def loads(g):
        wide = slice(g * HEADS_W, (g + 1) * HEADS_W)
        lanes = slice(g * HEAD_DIM, (g + 1) * HEAD_DIM)
        return (
            pltpu.make_async_copy(qs.at[0, :, wide], q_v.at[:, wide], loc.at[g, 0]),
            pltpu.make_async_copy(og.at[0, :, wide], g_v.at[:, wide], loc.at[g, 1]),
            pltpu.make_async_copy(ks.at[0, :, lanes], kwin.at[g, 1, 0], loc.at[g, 2]),
            pltpu.make_async_copy(vs.at[0, :, lanes], kwin.at[g, 1, 1], loc.at[g, 3]),
        )

    def hidden_cols(which):
        return hid.at[0, :, pl.ds(pl.multiple_of(which * QUARTER, 128), QUARTER)]

    own_h = pltpu.make_async_copy(hidden_cols(x), hall.at[0], loh)
    for g in range(KV_HEADS):
        for c in loads(g):
            c.start()
    own_h.start()

    eye = lax.broadcasted_iota(jnp.int32, (TOK, TOK), 0) == lax.broadcasted_iota(jnp.int32, (TOK, TOK), 1)
    own_row = docs[:, pl.ds(pl.multiple_of(ctx * TOK, TOK), TOK)].astype(F32)
    prv_row = docs[:, pl.ds(pl.multiple_of(prv * TOK, TOK), TOK)].astype(F32)
    prv_row = jnp.where(ctx == 0, -1.0, prv_row)

    def as_column(row):
        return jnp.sum(jnp.where(eye, jnp.broadcast_to(row, (TOK, TOK)), 0.0), axis=1, keepdims=True)

    earlier = lax.broadcasted_iota(jnp.int32, (TOK, TOK), 0) <= lax.broadcasted_iota(jnp.int32, (TOK, TOK), 1)
    bias[0:TOK, :] = jnp.where(as_column(prv_row) == own_row, 0.0, -1e30)
    bias[TOK:, :] = jnp.where(jnp.logical_and(as_column(own_row) == own_row, earlier), 0.0, -1e30)

    pl.semaphore_wait(barrier, greeted)

    def window(g):
        lanes = slice(g * HEAD_DIM, (g + 1) * HEAD_DIM)
        to = {"ctx": nxt, "fsdp": fsdp}
        return (
            remote(ks.at[0, :, lanes], kwin.at[g, 0, 0], kvs.at[g], kvr.at[g], to),
            remote(vs.at[0, :, lanes], kwin.at[g, 0, 1], kvs.at[g], kvr.at[g], to),
        )

    for g in range(KV_HEADS):
        for c in window(g):
            c.start()
    for dx in (2, 1, 3):
        remote(hidden_cols(lax.rem(x + dx, X)), hall.at[dx], hs.at[0], hr.at[0], x_dev(dx, 0)).start()
    remote(hidden_cols(x), hall.at[4], hs.at[1], hr.at[1], x_dev(0, 1)).start()

    def forward_hidden():
        wait_bytes(hall.at[1:4], hr.at[0])
        for dx in range(1, X):
            remote(hall.at[dx], hall.at[4 + dx], hs.at[1], hr.at[1], x_dev(0, 1)).start()

    def turn_hidden():
        own_h.wait()
        wait_bytes(hall.at[4:8], hr.at[1])
        for k in range(8):
            ht[:, k * TOK:(k + 1) * TOK] = hall[k].T

    scale = 1.0 / math.sqrt(HEAD_DIM)
    scale2 = scale * math.log2(math.e)

    def contribs(g):
        return remote(csend.at[g], crecv.at[g], cs.at[g], cr.at[g], {"ctx": prv, "fsdp": fsdp})

    def attention(g):
        for c in loads(g):
            c.wait()
        wait_bytes(kwin.at[g, 0], kvr.at[g])
        kw = jnp.concatenate([kwin[g, 0, 0], kwin[g, 1, 0]], axis=0)
        vw = jnp.concatenate([kwin[g, 0, 1], kwin[g, 1, 1]], axis=0)
        both = jnp.concatenate([bias[...], bias[...]], axis=1)
        for i in range(GROUP // 2):
            at = [slice((g * GROUP + 2 * i + j) * HEAD_DIM, (g * GROUP + 2 * i + j + 1) * HEAD_DIM) for j in range(2)]
            q2 = jnp.concatenate([q_v[:, at[0]], q_v[:, at[1]]], axis=0)
            g2 = jnp.concatenate([g_v[:, at[0]], g_v[:, at[1]]], axis=0)
            s = mm(kw, q2, ((1,), (1,))) * scale2 + both
            dp = mm(vw, g2, ((1,), (1,)))
            e = jnp.exp2(s - jnp.max(s, axis=0, keepdims=True))
            inv = 1.0 / jnp.sum(e, axis=0, keepdims=True)
            p = e * inv
            delta = jnp.sum(p * dp, axis=0, keepdims=True)
            cols = slice(2 * i * HEAD_DIM, 2 * (i + 1) * HEAD_DIM)
            dsb[:, cols] = (p * (dp - delta)).astype(BF16)
            pbb[:, cols] = p.astype(BF16)
            qst[cols, :] = q2
            gst[cols, :] = g2
        csend[g, 0] = mm(dsb[0:TOK, :], qst[...], ((1,), (0,))) * scale
        csend[g, 1] = mm(pbb[0:TOK, :], gst[...], ((1,), (0,)))
        contribs(g).start()
        cown[g, 0] = mm(dsb[TOK:, :], qst[...], ((1,), (0,))) * scale
        cown[g, 1] = mm(pbb[TOK:, :], gst[...], ((1,), (0,)))

    def out_copies(g):
        return [
            pltpu.make_async_copy(
                kvb.at[g, j], kv_out.at[0, :, j * KV_W + g * HEAD_DIM:j * KV_W + (g + 1) * HEAD_DIM], outs.at[2 * g + j]
            )
            for j in range(2)
        ]

    def finish(g):
        contribs(g).wait_recv()
        kvb[g] = (crecv[g] + cown[g]).astype(BF16)
        for k in (2, 6, 1, 3, 5, 7, 4):
            remote(
                kvb.at[g, lax.rem(core + k // 4, 2)], kall.at[g, k], xs.at[g], xr.at[g], x_dev(k % 4, k // 4)
            ).start()
        kall[g, 0] = kvb[g, core]
        for c in out_copies(g):
            c.start()

    def product(g):
        wait_bytes(kall.at[g, 1:8], xr.at[g])
        w = mm(ht[...], kall[g].reshape(8 * TOK, HEAD_DIM), ((1,), (0,))).reshape(Y, CHUNK, HEAD_DIM)
        wlo[g] = w.astype(BF16)
        for k in (4, 3, 5, 2, 6, 1, 7):
            remote(wlo.at[g, lax.rem(y + k, Y)], yrecv.at[g, k], ys.at[g], yr.at[g], y_dev(k)).start()
        w32[g] = w

    def z_copy(g, half):
        return remote(zsend.at[g, half], zrecv.at[z], zs.at[g, half], zr, owner(g, half))

    def is_mine(g, half):
        return jnp.logical_and(selfish, jnp.logical_and(x == g, core == half))

    def y_sum(g):
        wait_bytes(yrecv.at[g, 1:8], yr.at[g])
        total = w32[g, y]
        for k in range(1, Y):
            total = total + yrecv[g, k].astype(F32)
        zsend[g] = total.reshape(2, ROWS, HEAD_DIM)
        for half in range(2):
            mine = is_mine(g, half)

            @pl.when(mine)
            def _(half=half):
                pltpu.make_async_copy(zsend.at[g, half], zrecv.at[z], zr).start()

            @pl.when(jnp.logical_not(mine))
            def _(half=half):
                z_copy(g, half).start()

    attention(0)
    attention(1)
    attention(2)
    forward_hidden()
    finish(0)
    attention(3)
    finish(1)
    turn_hidden()
    finish(2)
    product(0)
    finish(3)
    product(1)
    product(2)
    y_sum(0)
    product(3)
    y_sum(1)
    y_sum(2)
    y_sum(3)

    wait_bytes(hall.at[1:4], hs.at[0])
    wait_bytes(hall.at[4:8], hs.at[1])
    for g in range(KV_HEADS):
        wait_bytes(kwin.at[g, 0], kvs.at[g])
        contribs(g).wait_send()
        wait_bytes(kall.at[g, 1:8], xs.at[g])
        wait_bytes(yrecv.at[g, 1:8], ys.at[g])
        for c in out_copies(g):
            c.wait()
        for half in range(2):
            @pl.when(jnp.logical_not(is_mine(g, half)))
            def _(half=half):
                z_copy(g, half).wait_send()

    wait_bytes(zrecv, zr)
    w = zrecv[0]
    for k in range(1, Z):
        w = w + zrecv[k]

    gpart[...] = mm(w, w, ((0,), (0,)), precision=HIGHEST).reshape(8, 16, HEAD_DIM)
    for k in (6, 7, 4, 5, 2, 3, 1):
        remote(gpart.at[lax.rem(cell + k, 8)], g1buf.at[k], g1s, g1r, cell_dev(k)).start()
    total = gpart[cell]
    wait_bytes(g1buf.at[1:8], g1r)
    for k in range(1, 8):
        total = total + g1buf[k]
    s1[...] = total
    for k in (4, 3, 5, 2, 6, 1, 7):
        remote(s1, g2buf.at[k], g2s, g2r, z_dev(k)).start()
    wait_bytes(g1buf.at[1:8], g1s)
    wait_bytes(g2buf.at[1:8], g2r)
    for k in range(1, 8):
        total = total + g2buf[k]
    gfull[cell] = total
    for k in (6, 7, 4, 5, 2, 3, 1):
        remote(gfull.at[cell], gfull.at[cell], g3s, g3r, cell_dev(k)).start()
    wait_bytes(g2buf.at[1:8], g2s)
    wait_bytes(g1buf.at[1:8], g3r)
    gram = gfull[...].reshape(HEAD_DIM, HEAD_DIM)

    ident = jnp.where(eye, 1.0, 0.0)
    norm = jnp.sqrt(jnp.sum(jnp.sum(gram * ident, axis=1, keepdims=True), axis=0, keepdims=True))
    inv = 1.0 / (norm + 1e-07)
    gram = gram * inv * inv

    def dot(a, b):
        return mm(a, b, ((1,), (0,)), precision=HIGHEST)

    run = None
    for it in range(NS_ITERS):
        poly = coeff_a * ident + coeff_b * gram + coeff_c * dot(gram, gram)
        run = poly if run is None else dot(run, poly)
        if it < NS_ITERS - 1:
            gram = dot(dot(poly, gram), poly)
    up_out[0] = dot(w * (inv * math.sqrt(D)), run)
    wait_bytes(g1buf.at[1:8], g3s)


def shards(hidden, queries, keys, values, out_grad, doc_ids):
    any_spec = pl.BlockSpec(memory_space=pl.ANY)
    vmem = pl.BlockSpec(memory_space=pltpu.VMEM)
    dma = pltpu.SemaphoreType.DMA
    heads = KV_HEADS
    return pl.pallas_call(
        kernel,
        out_shape=(
            jax.ShapeDtypeStruct((1, TOK, 2 * KV_W), BF16),
            jax.ShapeDtypeStruct((1, ROWS, HEAD_DIM), F32),
        ),
        in_specs=[any_spec] * 5 + [vmem],
        out_specs=(any_spec, vmem),
        scratch_shapes=[
            pltpu.VMEM((TOK, heads * HEADS_W), BF16),
            pltpu.VMEM((TOK, heads * HEADS_W), BF16),
            pltpu.VMEM((heads, 2, 2, TOK, HEAD_DIM), BF16),
            pltpu.VMEM((2 * TOK, TOK), F32),
            pltpu.VMEM((HEADS_W, HEAD_DIM), BF16),
            pltpu.VMEM((HEADS_W, HEAD_DIM), BF16),
            pltpu.VMEM((2 * TOK, HEADS_W), BF16),
            pltpu.VMEM((2 * TOK, HEADS_W), BF16),
            pltpu.VMEM((heads, 2, TOK, HEAD_DIM), F32),
            pltpu.VMEM((heads, 2, TOK, HEAD_DIM), F32),
            pltpu.VMEM((heads, 2, TOK, HEAD_DIM), F32),
            pltpu.VMEM((heads, 2, TOK, HEAD_DIM), BF16),
            pltpu.VMEM((8, TOK, QUARTER), BF16),
            pltpu.VMEM((QUARTER, 8 * TOK), BF16),
            pltpu.VMEM((heads, 8, TOK, HEAD_DIM), BF16),
            pltpu.VMEM((heads, Y, CHUNK, HEAD_DIM), F32),
            pltpu.VMEM((heads, Y, CHUNK, HEAD_DIM), BF16),
            pltpu.VMEM((heads, Y, CHUNK, HEAD_DIM), BF16),
            pltpu.VMEM((heads, 2, ROWS, HEAD_DIM), F32),
            pltpu.VMEM((Z, ROWS, HEAD_DIM), F32),
            pltpu.VMEM((8, 16, HEAD_DIM), F32),
            pltpu.VMEM((8, 16, HEAD_DIM), F32),
            pltpu.VMEM((16, HEAD_DIM), F32),
            pltpu.VMEM((8, 16, HEAD_DIM), F32),
            pltpu.VMEM((8, 16, HEAD_DIM), F32),
            dma((heads, 4)), dma,
            dma((heads,)), dma((heads,)),
            dma((2,)), dma((2,)),
            dma((heads,)), dma((heads,)),
            dma((heads,)), dma((heads,)),
            dma((heads,)), dma((heads,)),
            dma((heads, 2)), dma,
            dma, dma,
            dma, dma,
            dma, dma,
            dma((2 * heads,)),
        ],
        compiler_params=pltpu.CompilerParams(
            collective_id=0, has_side_effects=True, vmem_limit_bytes=56 * 1024 * 1024
        ),
        name="muon_kv_grads",
    )(hidden, queries, keys, values, out_grad, doc_ids)


def solution(mesh):
    placed = (P("fsdp", "ctx", None),) * 5 + (P("fsdp", None),)
    return jax.shard_map(
        shards,
        mesh=mesh,
        in_specs=placed,
        out_specs=(P("fsdp", "ctx", None), P("fsdp", "ctx", None)),
        check_vma=False,
    )
```

time: 92.6 us -> 78.4 us (0.85)
  Pallas kernels: 83.9 us -> 74.5 us
  local copies, waits for them, and re-layouts: 7.77 us -> 3 us
    pallas_call x1, Pallas kernels: 83.9 us -> 74.5 us  [shards(): pl.pallas_call(kernel, out_shape=(jax.ShapeDtypeStruct((1, TOK, 2 * KV_W)...]
    unnamed x14 -> x2, local copies, waits for them, and re-layouts: 7.77 us -> 3 us
where the time goes in v2:
time: 78.4 us; the launch traced here: 78.1 us
  Pallas kernels  74.5 us (95%)
  local copies, waits for them, and re-layouts  3 us (4%)
    pallas_call x1, Pallas kernels, shards(): pl.pallas_call(kernel, out_shape=(jax.ShapeDtypeStruct((1, TOK, 2 * KV_W)...  74.5 us
    unnamed x2, local copies, waits for them, and re-layouts  3 us

profile of v2, /device:TPU:7, one launch (start us, length us, event | category | flops | bytes accessed | tf_op | source)
XLA Modules:
  0.0 78.1 jit_solution(3456070840174293010)
XLA Ops:
  0.6 74.5 %muon_kv_grads.1 = (bf16[1,128,1024]{2,1,0:T(8,128)(2,1)}, f32[1,40,128]{2,1,0:T(8,128)}) custom-call(bf16[1,128,2560]{2,1,0:T(8,128)(2,1)} %hid.1, bf16[1,128,6144]{2,1,0:T(8,128)(2,1)} %qs.1, bf16[1,128,512]{2,1,0:T(8,128)(2,1)} %ks.1, bf16[1,128,512]{2,1,0:T(8,128)(2,1)} %vs.1, bf16[1,128,6144]{2,1,0:T(8,128)(2,1)} %og.1, s32[1,8192]{1,0:T(1,128)} %docs.1), custom_call_target="tpu_custom_call" | custom-call | tf_op jit(solution)/shard_map/muon_kv_grads/pallas_call | solution.py:328
  75.1 1.7 %copy.10 = bf16[1,128,1024]{2,1,0:T(8,128)(2,1)} copy(bf16[1,128,1024]{2,1,0:T(8,128)(2,1)} %get-tuple-element.4) | data formatting | bytes 524288
  76.8 1.3 %copy.11 = f32[1,40,128]{2,1,0:T(8,128)} copy(f32[1,40,128]{2,1,0:T(8,128)} %get-tuple-element.5) | data formatting | bytes 40960

commit v3 on v2

--- a/solution.py
+++ b/solution.py
@@ -52,7 +52,7 @@
     hid, qs, ks, vs, og, docs, kv_out, up_out,
     q_v, g_v, kwin, bias, qst, gst, dsb, pbb, csend, cown, crecv, kvb, hall, ht, kall, w32, wlo,
     yrecv, zsend, zrecv, gpart, g1buf, s1, g2buf, gfull,
-    loc, loh, kvs, kvr, hs, hr, cs, cr, xs, xr, ys, yr, zs, zr, g1s, g1r, g2s, g2r, g3s, g3r, outs,
+    word_y, word_z, loc, loh, kvs, kvr, hs, hr, cs, cr, xs, xr, ys, yr, zs, zr, g1s, g1r, g2s, g2r, g3s, g3r, outs,
 ):
     ctx, fsdp = lax.axis_index("ctx"), lax.axis_index("fsdp")
     z, yl, core = ctx // 8, lax.rem(ctx // 2, YL), lax.rem(ctx, 2)
@@ -74,10 +74,21 @@
     def z_dev(k):
         return {"ctx": lax.rem(z + k, Z) * 8 + cell, "fsdp": fsdp}
 
+    def first_dev(g, k):
+        return z_dev(k) if g % 2 else y_dev(k)
+
+    def place(g):
+        return z if g % 2 else y
+
     def owner(g, half):
-        return device(g, core, yl, 2 * x + yh, half)
-
-    selfish = jnp.logical_and(core == yh, z == 2 * x + yh)
+        where = place(g)
+        return device(g, core, lax.rem(where, YL), 2 * x + where // YL, half)
+
+    def is_mine(g, half):
+        where = place(g)
+        here = jnp.logical_and(yl == lax.rem(where, YL), z == 2 * x + where // YL)
+        return jnp.logical_and(jnp.logical_and(x == g, core == half), jnp.logical_and(core == yh, here))
+
     barrier = pltpu.get_barrier_semaphore()
 
     def greet(to):
@@ -90,15 +101,7 @@
         greet(y_dev(k))
         greet(cell_dev(k))
         greet(z_dev(k))
-    sources = [device(z // 2, lax.rem(z, 2), yl, lax.rem(z + k, Z), yh) for k in range(Z)]
-
-    @pl.when(jnp.logical_not(selfish))
-    def _():
-        greet(sources[0])
-
-    for src in sources[1:]:
-        greet(src)
-    greeted = 2 + 4 * 7 + Z - selfish.astype(jnp.int32)
+    greeted = 2 + 4 * 7
 
     def loads(g):
         wide = slice(g * HEADS_W, (g + 1) * HEADS_W)
@@ -114,10 +117,8 @@
         return hid.at[0, :, pl.ds(pl.multiple_of(which * QUARTER, 128), QUARTER)]
 
     own_h = pltpu.make_async_copy(hidden_cols(x), hall.at[0], loh)
-    for g in range(KV_HEADS):
-        for c in loads(g):
-            c.start()
-    own_h.start()
+    for c in loads(0):
+        c.start()
 
     eye = lax.broadcasted_iota(jnp.int32, (TOK, TOK), 0) == lax.broadcasted_iota(jnp.int32, (TOK, TOK), 1)
     own_row = docs[:, pl.ds(pl.multiple_of(ctx * TOK, TOK), TOK)].astype(F32)
@@ -147,6 +148,18 @@
     for dx in (2, 1, 3):
         remote(hidden_cols(lax.rem(x + dx, X)), hall.at[dx], hs.at[0], hr.at[0], x_dev(dx, 0)).start()
     remote(hidden_cols(x), hall.at[4], hs.at[1], hr.at[1], x_dev(0, 1)).start()
+    for g in range(1, KV_HEADS):
+        for c in loads(g):
+            c.start()
+    own_h.start()
+
+    for k in range(1, 8):
+        pl.semaphore_signal(word_y, inc=1, device_id=y_dev(k), device_id_type=MESH)
+
+    def pass_word():
+        pl.semaphore_wait(word_y, 7)
+        for k in range(1, 8):
+            pl.semaphore_signal(word_z, inc=1, device_id=z_dev(k), device_id_type=MESH)
 
     def forward_hidden():
         wait_bytes(hall.at[1:4], hr.at[0])
@@ -217,18 +230,15 @@
         w = mm(ht[...], kall[g].reshape(8 * TOK, HEAD_DIM), ((1,), (0,))).reshape(Y, CHUNK, HEAD_DIM)
         wlo[g] = w.astype(BF16)
         for k in (4, 3, 5, 2, 6, 1, 7):
-            remote(wlo.at[g, lax.rem(y + k, Y)], yrecv.at[g, k], ys.at[g], yr.at[g], y_dev(k)).start()
+            remote(wlo.at[g, lax.rem(place(g) + k, Y)], yrecv.at[g, k], ys.at[g], yr.at[g], first_dev(g, k)).start()
         w32[g] = w
 
     def z_copy(g, half):
-        return remote(zsend.at[g, half], zrecv.at[z], zs.at[g, half], zr, owner(g, half))
-
-    def is_mine(g, half):
-        return jnp.logical_and(selfish, jnp.logical_and(x == g, core == half))
+        return remote(zsend.at[g, half], zrecv.at[place(g + 1)], zs.at[g, half], zr, owner(g, half))
 
     def y_sum(g):
         wait_bytes(yrecv.at[g, 1:8], yr.at[g])
-        total = w32[g, y]
+        total = w32[g, place(g)]
         for k in range(1, Y):
             total = total + yrecv[g, k].astype(F32)
         zsend[g] = total.reshape(2, ROWS, HEAD_DIM)
@@ -237,7 +247,7 @@
 
             @pl.when(mine)
             def _(half=half):
-                pltpu.make_async_copy(zsend.at[g, half], zrecv.at[z], zr).start()
+                pltpu.make_async_copy(zsend.at[g, half], zrecv.at[place(g + 1)], zr).start()
 
             @pl.when(jnp.logical_not(mine))
             def _(half=half):
@@ -246,16 +256,18 @@
     attention(0)
     attention(1)
     attention(2)
-    forward_hidden()
     finish(0)
     attention(3)
     finish(1)
+    forward_hidden()
+    pass_word()
+    finish(2)
     turn_hidden()
-    finish(2)
     product(0)
     finish(3)
     product(1)
     product(2)
+    pl.semaphore_wait(word_z, 7)
     y_sum(0)
     product(3)
     y_sum(1)
@@ -320,17 +332,32 @@
     wait_bytes(g1buf.at[1:8], g3s)
 
 
+def write_results(kv, up, kv_out, up_out, kv_v, up_v, sems):
+    pairs = [(up.at[0], up_v, up_out.at[0], sems.at[4])]
+    for i in range(4):
+        rows = slice(i * 32, (i + 1) * 32)
+        pairs.append((kv.at[0, rows], kv_v.at[rows], kv_out.at[0, rows], sems.at[i]))
+    for src, mid, _, sem in pairs:
+        pltpu.make_async_copy(src, mid, sem).start()
+    for src, mid, dst, sem in pairs:
+        pltpu.make_async_copy(src, mid, sem).wait()
+        pltpu.make_async_copy(mid, dst, sem).start()
+    for _, mid, dst, sem in pairs:
+        pltpu.make_async_copy(mid, dst, sem).wait()
+
+
 def shards(hidden, queries, keys, values, out_grad, doc_ids):
     any_spec = pl.BlockSpec(memory_space=pl.ANY)
     vmem = pl.BlockSpec(memory_space=pltpu.VMEM)
     dma = pltpu.SemaphoreType.DMA
     heads = KV_HEADS
-    return pl.pallas_call(
+    out_shape = (
+        jax.ShapeDtypeStruct((1, TOK, 2 * KV_W), BF16),
+        jax.ShapeDtypeStruct((1, ROWS, HEAD_DIM), F32),
+    )
+    results = pl.pallas_call(
         kernel,
-        out_shape=(
-            jax.ShapeDtypeStruct((1, TOK, 2 * KV_W), BF16),
-            jax.ShapeDtypeStruct((1, ROWS, HEAD_DIM), F32),
-        ),
+        out_shape=out_shape,
         in_specs=[any_spec] * 5 + [vmem],
         out_specs=(any_spec, vmem),
         scratch_shapes=[
@@ -359,6 +386,7 @@
             pltpu.VMEM((16, HEAD_DIM), F32),
             pltpu.VMEM((8, 16, HEAD_DIM), F32),
             pltpu.VMEM((8, 16, HEAD_DIM), F32),
+            pltpu.SemaphoreType.REGULAR, pltpu.SemaphoreType.REGULAR,
             dma((heads, 4)), dma,
             dma((heads,)), dma((heads,)),
             dma((2,)), dma((2,)),
@@ -376,6 +404,19 @@
         ),
         name="muon_kv_grads",
     )(hidden, queries, keys, values, out_grad, doc_ids)
+    return pl.pallas_call(
+        write_results,
+        out_shape=out_shape,
+        in_specs=[any_spec] * 2,
+        out_specs=(any_spec, any_spec),
+        scratch_shapes=[
+            pltpu.VMEM((TOK, 2 * KV_W), BF16),
+            pltpu.VMEM((ROWS, HEAD_DIM), F32),
+            dma((5,)),
+        ],
+        compiler_params=pltpu.CompilerParams(vmem_limit_bytes=56 * 1024 * 1024),
+        name="write_results",
+    )(*results)
 
 
 def solution(mesh):

time: 78.4 us -> 78.6 us (level)
  Pallas kernels: 74.5 us -> 77.7 us
  local copies, waits for them, and re-layouts: 3 us -> 0 us
    pallas_call x1 -> x2, Pallas kernels: 74.5 us -> 77.7 us  [the longest x1 76.1 us: shards(): pl.pallas_call(kernel, out_shape=out_shape, in_specs=[any_spec] * 5 + [vm...]
    unnamed x2 -> x0, local copies, waits for them, and re-layouts: 3 us -> none
where the time goes in v3:
time: 78.6 us; the launch traced here: 78.4 us
  Pallas kernels  77.7 us (99%)
    pallas_call x1, Pallas kernels, shards(): pl.pallas_call(kernel, out_shape=out_shape, in_specs=[any_spec] * 5 + [vm...  76.1 us
    pallas_call x1, Pallas kernels, shards(): pl.pallas_call(write_results, out_shape=out_shape, in_specs=[any_spec] *...  1.62 us

profile of v3, /device:TPU:7, one launch (start us, length us, event | category | flops | bytes accessed | tf_op | source)
XLA Modules:
  0.0 78.4 jit_solution(3296839269920905089)
XLA Ops:
  0.6 76.1 %muon_kv_grads.1 = (bf16[1,128,1024]{2,1,0:T(8,128)(2,1)}, f32[1,40,128]{2,1,0:T(8,128)}) custom-call(bf16[1,128,2560]{2,1,0:T(8,128)(2,1)} %hid.1, bf16[1,128,6144]{2,1,0:T(8,128)(2,1)} %qs.1, bf16[1,128,512]{2,1,0:T(8,128)(2,1)} %ks.1, bf16[1,128,512]{2,1,0:T(8,128)(2,1)} %vs.1, bf16[1,128,6144]{2,1,0:T(8,128)(2,1)} %og.1, s32[1,8192]{1,0:T(1,128)} %docs.1), custom_call_target="tpu_custom_call" | custom-call | tf_op jit(solution)/shard_map/muon_kv_grads/pallas_call | solution.py:358
  76.8 1.6 %write_results.1 = (bf16[1,128,1024]{2,1,0:T(8,128)(2,1)}, f32[1,40,128]{2,1,0:T(8,128)}) custom-call(bf16[1,128,1024]{2,1,0:T(8,128)(2,1)} %get-tuple-element.4.kv, f32[1,40,128]{2,1,0:T(8,128)} %get-tuple-element.5.up), custom_call_target="tpu_custom_call" | custom-call | tf_op jit(solution)/shard_map/write_results/pallas_call | solution.py:407

commit v4 on v3

--- a/solution.py
+++ b/solution.py
@@ -19,6 +19,7 @@
 ROWS = CHUNK // 2
 HEADS_W = GROUP * HEAD_DIM
 KV_W = KV_HEADS * HEAD_DIM
+Z_FIRST = (1,)
 
 coeff_a = 3.4445
 coeff_b = -4.775
@@ -75,10 +76,10 @@
         return {"ctx": lax.rem(z + k, Z) * 8 + cell, "fsdp": fsdp}
 
     def first_dev(g, k):
-        return z_dev(k) if g % 2 else y_dev(k)
+        return z_dev(k) if g in Z_FIRST else y_dev(k)
 
     def place(g):
-        return z if g % 2 else y
+        return z if g in Z_FIRST else y
 
     def owner(g, half):
         where = place(g)
@@ -88,6 +89,9 @@
         where = place(g)
         here = jnp.logical_and(yl == lax.rem(where, YL), z == 2 * x + where // YL)
         return jnp.logical_and(jnp.logical_and(x == g, core == half), jnp.logical_and(core == yh, here))
+
+    def owner_slot(g):
+        return y if g in Z_FIRST else z
 
     barrier = pltpu.get_barrier_semaphore()
 
@@ -234,7 +238,7 @@
         w32[g] = w
 
     def z_copy(g, half):
-        return remote(zsend.at[g, half], zrecv.at[place(g + 1)], zs.at[g, half], zr, owner(g, half))
+        return remote(zsend.at[g, half], zrecv.at[owner_slot(g)], zs.at[g, half], zr, owner(g, half))
 
     def y_sum(g):
         wait_bytes(yrecv.at[g, 1:8], yr.at[g])
@@ -247,7 +251,7 @@
 
             @pl.when(mine)
             def _(half=half):
-                pltpu.make_async_copy(zsend.at[g, half], zrecv.at[place(g + 1)], zr).start()
+                pltpu.make_async_copy(zsend.at[g, half], zrecv.at[owner_slot(g)], zr).start()
 
             @pl.when(jnp.logical_not(mine))
             def _(half=half):
@@ -255,24 +259,22 @@
 
     attention(0)
     attention(1)
+    finish(0)
     attention(2)
-    finish(0)
-    attention(3)
     finish(1)
     forward_hidden()
-    pass_word()
+    attention(3)
     finish(2)
     turn_hidden()
+    pass_word()
     product(0)
     finish(3)
     product(1)
     product(2)
+    product(3)
     pl.semaphore_wait(word_z, 7)
-    y_sum(0)
-    product(3)
-    y_sum(1)
-    y_sum(2)
-    y_sum(3)
+    for g in range(KV_HEADS):
+        y_sum(g)
 
     wait_bytes(hall.at[1:4], hs.at[0])
     wait_bytes(hall.at[4:8], hs.at[1])
@@ -319,16 +321,32 @@
     inv = 1.0 / (norm + 1e-07)
     gram = gram * inv * inv
 
+    def parts(v):
+        high = v.astype(BF16)
+        rest = v - high.astype(F32)
+        mid = rest.astype(BF16)
+        return high, mid, (rest - mid.astype(F32)).astype(BF16)
+
+    def left(p):
+        return jnp.concatenate([p[2], p[0], p[1], p[1], p[0], p[0]], axis=1)
+
+    def right(p):
+        return jnp.concatenate([p[0], p[2], p[1], p[0], p[1], p[0]], axis=0)
+
     def dot(a, b):
-        return mm(a, b, ((1,), (0,)), precision=HIGHEST)
-
-    run = None
+        return mm(a, b, ((1,), (0,)))
+
+    state = w * inv
     for it in range(NS_ITERS):
-        poly = coeff_a * ident + coeff_b * gram + coeff_c * dot(gram, gram)
-        run = poly if run is None else dot(run, poly)
+        gram_parts = parts(gram)
+        gram_right = right(gram_parts)
+        poly = coeff_a * ident + coeff_b * gram + coeff_c * dot(left(gram_parts), gram_right)
+        poly_parts = parts(poly)
+        poly_right = right(poly_parts)
         if it < NS_ITERS - 1:
-            gram = dot(dot(poly, gram), poly)
-    up_out[0] = dot(w * (inv * math.sqrt(D)), run)
+            gram = dot(left(parts(dot(left(poly_parts), gram_right))), poly_right)
+        state = dot(left(parts(state)), poly_right)
+    up_out[0] = math.sqrt(D) * state
     wait_bytes(g1buf.at[1:8], g3s)
 
 

time: 78.6 us -> 71.8 us (0.913)
  Pallas kernels: 77.7 us -> 70.7 us
    pallas_call x1, Pallas kernels: 76.1 us -> 69.1 us  [shards(): pl.pallas_call(kernel, out_shape=out_shape, in_specs=[any_spec] * 5 + [vm...]
where the time goes in v4:
time: 71.8 us; the launch traced here: 71.3 us
  Pallas kernels  70.7 us (98%)
    pallas_call x1, Pallas kernels, shards(): pl.pallas_call(kernel, out_shape=out_shape, in_specs=[any_spec] * 5 + [vm...  69.1 us
    pallas_call x1, Pallas kernels, shards(): pl.pallas_call(write_results, out_shape=out_shape, in_specs=[any_spec] *...  1.62 us

profile of v4, /device:TPU:7, one launch (start us, length us, event | category | flops | bytes accessed | tf_op | source)
XLA Modules:
  0.0 71.3 jit_solution(3546326547535024411)
XLA Ops:
  0.6 69.1 %muon_kv_grads.1 = (bf16[1,128,1024]{2,1,0:T(8,128)(2,1)}, f32[1,40,128]{2,1,0:T(8,128)}) custom-call(bf16[1,128,2560]{2,1,0:T(8,128)(2,1)} %hid.1, bf16[1,128,6144]{2,1,0:T(8,128)(2,1)} %qs.1, bf16[1,128,512]{2,1,0:T(8,128)(2,1)} %ks.1, bf16[1,128,512]{2,1,0:T(8,128)(2,1)} %vs.1, bf16[1,128,6144]{2,1,0:T(8,128)(2,1)} %og.1, s32[1,8192]{1,0:T(1,128)} %docs.1), custom_call_target="tpu_custom_call" | custom-call | tf_op jit(solution)/shard_map/muon_kv_grads/pallas_call | solution.py:376
  69.7 1.6 %write_results.1 = (bf16[1,128,1024]{2,1,0:T(8,128)(2,1)}, f32[1,40,128]{2,1,0:T(8,128)}) custom-call(bf16[1,128,1024]{2,1,0:T(8,128)(2,1)} %get-tuple-element.4.kv, f32[1,40,128]{2,1,0:T(8,128)} %get-tuple-element.5.up), custom_call_target="tpu_custom_call" | custom-call | tf_op jit(solution)/shard_map/write_results/pallas_call | solution.py:425

commit v5 on v4

--- a/solution.py
+++ b/solution.py
@@ -179,8 +179,8 @@
     scale = 1.0 / math.sqrt(HEAD_DIM)
     scale2 = scale * math.log2(math.e)
 
-    def contribs(g):
-        return remote(csend.at[g], crecv.at[g], cs.at[g], cr.at[g], {"ctx": prv, "fsdp": fsdp})
+    def contrib(g, j):
+        return remote(csend.at[g, j], crecv.at[g, j], cs.at[g], cr.at[g], {"ctx": prv, "fsdp": fsdp})
 
     def attention(g):
         for c in loads(g):
@@ -205,8 +205,9 @@
             qst[cols, :] = q2
             gst[cols, :] = g2
         csend[g, 0] = mm(dsb[0:TOK, :], qst[...], ((1,), (0,))) * scale
+        contrib(g, 0).start()
         csend[g, 1] = mm(pbb[0:TOK, :], gst[...], ((1,), (0,)))
-        contribs(g).start()
+        contrib(g, 1).start()
         cown[g, 0] = mm(dsb[TOK:, :], qst[...], ((1,), (0,))) * scale
         cown[g, 1] = mm(pbb[TOK:, :], gst[...], ((1,), (0,)))
 
@@ -219,7 +220,7 @@
         ]
 
     def finish(g):
-        contribs(g).wait_recv()
+        wait_bytes(crecv.at[g], cr.at[g])
         kvb[g] = (crecv[g] + cown[g]).astype(BF16)
         for k in (2, 6, 1, 3, 5, 7, 4):
             remote(
@@ -266,21 +267,23 @@
     attention(3)
     finish(2)
     turn_hidden()
+    product(0)
     pass_word()
-    product(0)
+    product(1)
     finish(3)
-    product(1)
     product(2)
+    pl.semaphore_wait(word_z, 7)
+    y_sum(0)
     product(3)
-    pl.semaphore_wait(word_z, 7)
-    for g in range(KV_HEADS):
-        y_sum(g)
+    y_sum(1)
+    y_sum(2)
+    y_sum(3)
 
     wait_bytes(hall.at[1:4], hs.at[0])
     wait_bytes(hall.at[4:8], hs.at[1])
     for g in range(KV_HEADS):
         wait_bytes(kwin.at[g, 0], kvs.at[g])
-        contribs(g).wait_send()
+        wait_bytes(crecv.at[g], cs.at[g])
         wait_bytes(kall.at[g, 1:8], xs.at[g])
         wait_bytes(yrecv.at[g, 1:8], ys.at[g])
         for c in out_copies(g):

time: 71.8 us -> 71.1 us (level)
  no operation moved by 1% of the time
where the time goes in v5:
time: 71.1 us; the launch traced here: 70.8 us
  Pallas kernels  70.2 us (99%)
    pallas_call x1, Pallas kernels, shards(): pl.pallas_call(kernel, out_shape=out_shape, in_specs=[any_spec] * 5 + [vm...  68.6 us
    pallas_call x1, Pallas kernels, shards(): pl.pallas_call(write_results, out_shape=out_shape, in_specs=[any_spec] *...  1.62 us

profile of v5, /device:TPU:7, one launch (start us, length us, event | category | flops | bytes accessed | tf_op | source)
XLA Modules:
  0.0 70.8 jit_solution(3658371169901292858)
XLA Ops:
  0.6 68.6 %muon_kv_grads.1 = (bf16[1,128,1024]{2,1,0:T(8,128)(2,1)}, f32[1,40,128]{2,1,0:T(8,128)}) custom-call(bf16[1,128,2560]{2,1,0:T(8,128)(2,1)} %hid.1, bf16[1,128,6144]{2,1,0:T(8,128)(2,1)} %qs.1, bf16[1,128,512]{2,1,0:T(8,128)(2,1)} %ks.1, bf16[1,128,512]{2,1,0:T(8,128)(2,1)} %vs.1, bf16[1,128,6144]{2,1,0:T(8,128)(2,1)} %og.1, s32[1,8192]{1,0:T(1,128)} %docs.1), custom_call_target="tpu_custom_call" | custom-call | tf_op jit(solution)/shard_map/muon_kv_grads/pallas_call | solution.py:379
  69.2 1.6 %write_results.1 = (bf16[1,128,1024]{2,1,0:T(8,128)(2,1)}, f32[1,40,128]{2,1,0:T(8,128)}) custom-call(bf16[1,128,1024]{2,1,0:T(8,128)(2,1)} %get-tuple-element.4.kv, f32[1,40,128]{2,1,0:T(8,128)} %get-tuple-element.5.up), custom_call_target="tpu_custom_call" | custom-call | tf_op jit(solution)/shard_map/write_results/pallas_call | solution.py:428

commit v6 on v5

--- a/solution.py
+++ b/solution.py
@@ -204,9 +204,9 @@
             pbb[:, cols] = p.astype(BF16)
             qst[cols, :] = q2
             gst[cols, :] = g2
-        csend[g, 0] = mm(dsb[0:TOK, :], qst[...], ((1,), (0,))) * scale
+        csend[g, 0] = (mm(dsb[0:TOK, :], qst[...], ((1,), (0,))) * scale).astype(BF16)
         contrib(g, 0).start()
-        csend[g, 1] = mm(pbb[0:TOK, :], gst[...], ((1,), (0,)))
+        csend[g, 1] = mm(pbb[0:TOK, :], gst[...], ((1,), (0,))).astype(BF16)
         contrib(g, 1).start()
         cown[g, 0] = mm(dsb[TOK:, :], qst[...], ((1,), (0,))) * scale
         cown[g, 1] = mm(pbb[TOK:, :], gst[...], ((1,), (0,)))
@@ -221,7 +221,7 @@
 
     def finish(g):
         wait_bytes(crecv.at[g], cr.at[g])
-        kvb[g] = (crecv[g] + cown[g]).astype(BF16)
+        kvb[g] = (crecv[g].astype(F32) + cown[g]).astype(BF16)
         for k in (2, 6, 1, 3, 5, 7, 4):
             remote(
                 kvb.at[g, lax.rem(core + k // 4, 2)], kall.at[g, k], xs.at[g], xr.at[g], x_dev(k % 4, k // 4)
@@ -390,9 +390,9 @@
             pltpu.VMEM((HEADS_W, HEAD_DIM), BF16),
             pltpu.VMEM((2 * TOK, HEADS_W), BF16),
             pltpu.VMEM((2 * TOK, HEADS_W), BF16),
+            pltpu.VMEM((heads, 2, TOK, HEAD_DIM), BF16),
             pltpu.VMEM((heads, 2, TOK, HEAD_DIM), F32),
-            pltpu.VMEM((heads, 2, TOK, HEAD_DIM), F32),
-            pltpu.VMEM((heads, 2, TOK, HEAD_DIM), F32),
+            pltpu.VMEM((heads, 2, TOK, HEAD_DIM), BF16),
             pltpu.VMEM((heads, 2, TOK, HEAD_DIM), BF16),
             pltpu.VMEM((8, TOK, QUARTER), BF16),
             pltpu.VMEM((QUARTER, 8 * TOK), BF16),

time: 71.1 us -> 70.8 us (level)
  no operation moved by 1% of the time
where the time goes in v6:
time: 70.8 us; the launch traced here: 70.6 us
  Pallas kernels  69.9 us (99%)
    pallas_call x1, Pallas kernels, shards(): pl.pallas_call(kernel, out_shape=out_shape, in_specs=[any_spec] * 5 + [vm...  68.3 us
    pallas_call x1, Pallas kernels, shards(): pl.pallas_call(write_results, out_shape=out_shape, in_specs=[any_spec] *...  1.62 us

profile of v6, /device:TPU:7, one launch (start us, length us, event | category | flops | bytes accessed | tf_op | source)
XLA Modules:
  0.0 70.6 jit_solution(11407582288896411225)
XLA Ops:
  0.6 68.3 %muon_kv_grads.1 = (bf16[1,128,1024]{2,1,0:T(8,128)(2,1)}, f32[1,40,128]{2,1,0:T(8,128)}) custom-call(bf16[1,128,2560]{2,1,0:T(8,128)(2,1)} %hid.1, bf16[1,128,6144]{2,1,0:T(8,128)(2,1)} %qs.1, bf16[1,128,512]{2,1,0:T(8,128)(2,1)} %ks.1, bf16[1,128,512]{2,1,0:T(8,128)(2,1)} %vs.1, bf16[1,128,6144]{2,1,0:T(8,128)(2,1)} %og.1, s32[1,8192]{1,0:T(1,128)} %docs.1), custom_call_target="tpu_custom_call" | custom-call | tf_op jit(solution)/shard_map/muon_kv_grads/pallas_call | solution.py:379
  68.9 1.6 %write_results.1 = (bf16[1,128,1024]{2,1,0:T(8,128)(2,1)}, f32[1,40,128]{2,1,0:T(8,128)}) custom-call(bf16[1,128,1024]{2,1,0:T(8,128)(2,1)} %get-tuple-element.4.kv, f32[1,40,128]{2,1,0:T(8,128)} %get-tuple-element.5.up), custom_call_target="tpu_custom_call" | custom-call | tf_op jit(solution)/shard_map/write_results/pallas_call | solution.py:428
